TPU v7x, 512 devices: a whole 4x4x16 slice. The times are simulated.
512 devices in a mesh: rep: 32 (over y, z_hi, core), exp: 16 (over z_lo, x).
Axes of the slice: x: 4, y: 4, z: 16 (z_hi: 4, z_lo: 4; z = z_hi * 4 + z_lo), core: 2. Of those that a mesh axis runs over, the one named last changes fastest.
Arguments:
- tokens: bfloat16 [32, 2048, 1024], P('rep', 'exp'), may hold values from -6 to 6
- cotangent: bfloat16 [32, 2048, 1024], P('rep', 'exp'), may hold values from -4 to 4
- route_ids: int32 [32, 2048, 2], P('rep', 'exp'), may hold values from 0 to 3, all different within a row; in each aligned block of 128 rows (0 to 127, 128 to 255, ..., all dimensions but the last counted through in order) at most 96 rows name the same one
- route_weights: bfloat16 [32, 2048, 2], P('rep', 'exp'), may hold values from 0.19921875 to 1
- gate_weight: bfloat16 [32, 1024, 5632], P('rep', None, 'exp'), may hold values from -0.1875 to 0.1875
- up_weight: bfloat16 [32, 1024, 5632], P('rep', None, 'exp'), may hold values from -0.1875 to 0.1875
- down_weight: bfloat16 [32, 5632, 1024], P('rep', 'exp'), may hold values from -0.15625 to 0.15625
- tracker: bfloat16 [32, 5632, 1024], P('rep', 'exp'), may hold values from -12 to 12
- grad_prev: bfloat16 [32, 5632, 1024], P('rep', 'exp'), may hold values from -12 to 12
- gossip_step: int32 [3], replicated, may hold values from 0 to 2
Outputs:
- token_grad: bfloat16 [32, 2048, 1024], P('rep', 'exp')
- tracker_new: bfloat16 [32, 5632, 1024], P('rep', 'exp')
Inputs may be any that keep to these rules, and one draw needn't show every extreme that they name: `route_ids`: each token names 2 different experts; within each aligned block of 128 tokens of a replica no expert is named by more than 96 tokens, and in some block one expert is named by exactly 96.
All inputs are finite; a program needn't handle non-finite values.
Results may differ from a plain program's by a relative error of at most 0.0058.
Values may be sent and summed in bfloat16 or wider, within the bound.
A program may use at most 64 MiB of HBM per device.

v0:
```python
from functools import partial

import jax
import jax.numpy as jnp
from jax import lax
from jax.experimental import pallas as pl
from jax.experimental.pallas import tpu as pltpu
from jax.sharding import PartitionSpec as P

D = 1024
EXPERTS = 4
ROUNDS = 3
TOK = 128
CAP = 96
WIDE = 256
HID = 352
COLS = 4 * CAP
ORDER = (1, 3, 2)
CHUNKS = ((0, 96), (96, 96), (192, 80), (272, 80))
LATE = ((0,), (1,), (2,), (0, 1), (0, 2), (1, 0), (1, 2), (2, 0), (2, 1))
ALL = [(a, b, c) for a in range(3) for b in range(3) for c in range(3)]
CHOICES = (
    [0 if a in (b, c) else a + 1 for a, b, c in ALL],
    [LATE.index((b,) if b == c else (b, c)) for a, b, c in ALL],
)
F32 = jnp.float32
BF16 = jnp.bfloat16
NT = (((1,), (1,)), ((), ()))
TN = (((0,), (0,)), ((), ()))
NN = (((1,), (0,)), ((), ()))


def dot(a, b, dims=NN):
    return lax.dot_general(a, b, dims, preferred_element_type=F32)


def layer_kernel(
    late,
    tok_ref,
    cot_ref,
    ids_ref,
    wts_ref,
    gate_ref,
    up_ref,
    down_ref,
    tracker_ref,
    peer_ref,
    prev_ref,
    out_ref,
    new_ref,
    stage,
    spread,
    rows,
    weights,
    gu,
    hd,
    gug,
    wtd,
    part,
    grads,
    gsend,
    grecv,
    psend,
    precv,
    ret,
    zsend,
    msend,
    mrecv,
    kept,
    z_ss,
    z_rs,
    a_ss,
    a_rs,
    w_ss,
    w_rs,
    g_ss,
    g_rs,
    p_ss,
    p_rs,
    r_ss,
    r_rs,
    m_ss,
    m_rs,
    own_sem,
    kept_sem,
):
    rep = lax.axis_index("rep")
    e = lax.axis_index("exp")
    z = e // 4
    x = e - 4 * z
    odd = x % 2
    pair = e + 1 - 2 * odd
    mate = 4 * z + (x + 3 + 2 * odd) % 4

    def at_z(d):
        return 4 * ((z + d) % 4) + x

    def across(bit):
        step = 2**bit
        return rep + step * (1 - 2 * ((rep // step) % 2))

    def send(src, dst, ss, rs, to, replica=None):
        return pltpu.make_async_remote_copy(
            src_ref=src,
            dst_ref=dst,
            send_sem=ss,
            recv_sem=rs,
            device_id=(rep if replica is None else replica, to),
            device_id_type=pl.DeviceIdType.MESH,
        )

    own = [
        pltpu.make_async_copy(ref, weights.at[0, pl.ds(i * HID, HID)], own_sem.at[i])
        for i, ref in enumerate((gate_ref, up_ref, down_ref))
    ]
    keep = [
        pltpu.make_async_copy(ref, kept.at[i], kept_sem.at[i])
        for i, ref in enumerate((tracker_ref, peer_ref, prev_ref))
    ]
    barrier = pltpu.get_barrier_semaphore()
    peers = [(rep, at_z(1)), (rep, at_z(2)), (rep, at_z(3)), (rep, pair), (rep, mate)]
    peers += [(across(bit), e) for bit in late]
    for to in peers:
        pl.semaphore_signal(
            barrier, inc=1, device_id=to, device_id_type=pl.DeviceIdType.MESH
        )
    for copy in own:
        copy.start()

    lane = lax.broadcasted_iota(jnp.int32, (TOK, TOK), 1)
    sub = lax.broadcasted_iota(jnp.int32, (TOK, TOK), 0)
    before = (sub < lane).astype(F32).astype(BF16)
    expert = lax.broadcasted_iota(jnp.int32, (8, TOK), 0)
    slot = lax.broadcasted_iota(jnp.int32, (CAP, TOK), 0).astype(F32)
    ids = ids_ref[...]
    wts = wts_ref[...].astype(F32)
    hit0 = (expert == ids[0:1]).astype(F32)
    hit1 = (expert == ids[1:2]).astype(F32)
    hit_t = hit0 + hit1
    coef_t = hit0 * wts[0:1] + hit1 * wts[1:2]
    rank_t = dot(hit_t.astype(BF16), before)

    def place(d):
        mine = expert == (z + d) % 4
        zero = jnp.zeros((8, TOK), F32)
        hit = jnp.sum(jnp.where(mine, hit_t, zero), axis=0, keepdims=True)
        rank = jnp.sum(jnp.where(mine, rank_t, zero), axis=0, keepdims=True)
        coef = jnp.sum(jnp.where(mine, coef_t, zero), axis=0, keepdims=True)
        placed = jnp.where(slot == rank, 1.0, 0.0) * hit
        plain = placed.astype(BF16)
        spread[pl.ds(pl.multiple_of(d * CAP, 16), CAP)] = plain
        t = dot(plain, tok_ref[...]).astype(BF16)
        c = dot((placed * coef).astype(BF16), cot_ref[...]).astype(BF16)
        return t, c

    def w_copy(i):
        piece = pl.ds(i * HID, HID)
        return send(weights.at[0, piece], weights.at[1, piece], w_ss.at[i], w_rs.at[i], mate)

    def z_copy(d):
        return send(stage.at[d], rows.at[0, :, z], z_ss.at[d], z_rs.at[d], at_z(d))

    def z_arrive(d):
        return send(stage.at[d], rows.at[0, :, (z + 4 - d) % 4], z_ss.at[d], z_rs.at[d], at_z(d))

    def a_copy(d):
        zs = (z + 4 - d) % 4
        return send(rows.at[0, :, zs], rows.at[1, :, zs], a_ss.at[d], a_rs.at[d], pair)

    pl.semaphore_wait(barrier, len(peers))
    for i in range(2):
        own[i].wait()
        w_copy(i).start()
    def place_step(i, carry):
        d = (2 * i + 1 - i // 2) % 4
        t, c = place(d)

        @pl.when(d == 0)
        def _():
            rows[0, 0, z] = t
            rows[0, 1, z] = c
            a_copy(0).start()

        @pl.when(d != 0)
        def _():
            stage[d, 0] = t
            stage[d, 1] = c

        @pl.when(i < 2)
        def _():
            z_copy(d).start()

        return carry

    lax.fori_loop(0, 4, place_step, 0)
    own[2].wait()
    for copy in keep:
        copy.start()

    z_copy(1).wait_send()
    z_copy(3).wait_send()
    z_copy(2).start()
    for d in ORDER:
        if d == 2:
            w_copy(0).wait_send()
            w_copy(1).wait_send()
            w_copy(2).start()
        z_arrive(d).wait_recv()
        a_copy(d).start()

    def chunk(c):
        return pl.ds(CHUNKS[c][0], CHUNKS[c][1])

    def g_copy(c):
        at = chunk(c)
        return send(gsend.at[at], grecv.at[at], g_ss.at[c], g_rs.at[c], mate)

    def m_copy(i, c):
        at = chunk(c)
        return send(
            msend.at[i, at], mrecv.at[i, at], m_ss.at[i, c], m_rs.at[i, c], e, across(late[i])
        )

    def each_tile(start, count, step, body):
        def run(i, carry):
            body(pl.ds(pl.multiple_of(start + i * step, 16), step))
            return carry

        lax.fori_loop(0, count, run, 0)

    def grad_step(n, carry):
        rg = n // 2
        hs = (n + rg) % 2

        @pl.when(n == 1)
        def _():
            w_copy(0).wait_recv()
            w_copy(1).wait_recv()

        @pl.when(n == 2)
        def _():
            for d in range(4):
                a_copy(d).wait_recv()

        def project(i, carry):
            piece = pl.ds(pl.multiple_of(i * HID, 16), HID)
            gu[2 * rg + hs, piece] = dot(weights[hs, piece], rows[rg, 0].reshape(COLS, D), NT)
            return carry

        lax.fori_loop(0, 2, project, 0)

        def body(at):
            g = gu[2 * rg + hs, at]
            u = gu[2 * rg + hs, pl.ds(at.start + HID, at.size)]
            wtd[at] = (g * jax.nn.sigmoid(g) * u).astype(BF16)

        each_tile(0, HID // 32, 32, body)
        def accumulate(i, carry):
            at = pl.ds(pl.multiple_of(i * WIDE, WIDE), WIDE)
            share = dot(wtd[...], rows[rg, 1, :, :, at].reshape(COLS, WIDE))

            @pl.when(n < 2)
            def _():
                grads[hs, :, at] = share

            @pl.when(n >= 2)
            def _():
                grads[hs, :, at] += share

            return carry

        lax.fori_loop(0, D // WIDE, accumulate, 0)

        @pl.when(n == 2)
        def _():
            def ready(at):
                gsend[at] = grads[1, at].astype(BF16)

            each_tile(0, HID // 16, 16, ready)
            g_copy(0).start()
            g_copy(1).start()

        return carry

    lax.fori_loop(0, 4, grad_step, 0)
    for copy in keep:
        copy.wait()

    def begin(at):
        share = (grads[0, at] + grecv[at].astype(F32) - kept[2, at].astype(F32)) / ROUNDS
        mixed = (kept[0, at].astype(F32) + kept[1, at].astype(F32)) * 0.5
        mixed = mixed + (share if len(late) == 2 else 2.0 * share)
        grads[0, at] = share
        grads[1, at] = mixed
        msend[0, at] = mixed.astype(BF16)

    for c, (start, size) in enumerate(CHUNKS):
        if c + 2 < len(CHUNKS):
            g_copy(c).wait_send()
            g_copy(c + 2).start()
        g_copy(c).wait_recv()
        each_tile(start, size // 16, 16, begin)
        m_copy(0, c).start()

    def mixed_by(i, at):
        return (grads[1, at] + mrecv[i, at].astype(F32)) * 0.5 + grads[0, at]

    def pass_on():
        def body(at):
            mixed = mixed_by(0, at)
            grads[1, at] = mixed
            msend[1, at] = mixed.astype(BF16)

        for c, (start, size) in enumerate(CHUNKS):
            m_copy(0, c).wait_recv()
            each_tile(start, size // 16, 16, body)
            m_copy(1, c).start()

    if len(late) == 2 and late[0] == 0:
        pass_on()

    def p_copy(d):
        zs = (z + d) % 4
        return send(psend.at[zs], precv.at[zs], p_ss.at[d], p_rs.at[d], pair)

    w_copy(2).wait_recv()

    def input_step(n, carry):
        rg = 1 - n // 2
        hs = n % 2
        hd[...] = dot(weights[hs, 2 * HID:3 * HID], rows[rg, 1].reshape(COLS, D), NT)

        def body(at):
            low = pl.ds(at.start + HID, at.size)
            g = gu[2 * rg + hs, at]
            u = gu[2 * rg + hs, low]
            h = hd[at]
            s = jax.nn.sigmoid(g)
            gug[at] = (h * u * s * (1.0 + g * (1.0 - s))).astype(BF16)
            gug[low] = (h * (g * s)).astype(BF16)

        each_tile(0, HID // 32, 32, body)
        def accumulate(i, carry):
            at = pl.ds(pl.multiple_of(i * WIDE, WIDE), WIDE)
            share = dot(gug[...], weights[hs, 0:2 * HID, at], TN)

            @pl.when(hs == 0)
            def _():
                part[:, at] = share

            @pl.when(hs == 1)
            def _():
                part[:, at] += share

            return carry

        lax.fori_loop(0, D // WIDE, accumulate, 0)

        @pl.when(n == 1)
        def _():
            def ready(at):
                psend[(at.start // CAP), pl.ds(at.start % CAP, 16)] = part[at].astype(BF16)

            each_tile(0, COLS // 16, 16, ready)
            p_copy(2).start()
            p_copy(1).start()

        return carry

    lax.fori_loop(0, 4, input_step, 0)
    p_copy(2).wait_send()
    p_copy(3).start()
    p_copy(1).wait_send()
    p_copy(0).start()

    def r_copy(d):
        return send(zsend.at[d], ret.at[4 - d], r_ss.at[d], r_rs.at[4 - d], at_z(d))

    for d in (2, 1, 3, 0):
        p_copy(d).wait_recv()
        zs = (z + d) % 4
        to = ret if d == 0 else zsend

        def add(at):
            mine = part[pl.ds(pl.multiple_of(zs * CAP + at.start, 16), 16)]
            to[d, at] = (mine + precv[zs, at].astype(F32)).astype(BF16)

        each_tile(0, CAP // 16, 16, add)
        if d != 0:
            r_copy(d).start()

    if len(late) == 2 and late[0] != 0:
        pass_on()
    for d in (1, 3, 2):
        r_copy(d).wait_recv()

    def collect(i, carry):
        at = pl.ds(pl.multiple_of(i * WIDE, WIDE), WIDE)
        found = dot(spread[...], ret[:, :, at].reshape(COLS, WIDE), TN)
        out_ref[:, at] = found.astype(BF16)
        return carry

    lax.fori_loop(0, D // WIDE, collect, 0)
    last = len(late) - 1

    def finish(at):
        new_ref[at] = mixed_by(last, at).astype(BF16)

    for c, (start, size) in enumerate(CHUNKS):
        m_copy(last, c).wait_recv()
        each_tile(start, size // 16, 16, finish)

    z_copy(2).wait_send()
    p_copy(3).wait_send()
    p_copy(0).wait_send()
    for d in (1, 2, 3):
        r_copy(d).wait_send()
    for d in range(4):
        a_copy(d).wait_send()
    w_copy(2).wait_send()
    for c in range(len(CHUNKS)):
        if c >= len(CHUNKS) - 2:
            g_copy(c).wait_send()
        for i in range(len(late)):
            m_copy(i, c).wait_send()


def layer(late, number, *arrays):
    vmem = pl.BlockSpec(memory_space=pltpu.VMEM)
    hbm = pl.BlockSpec(memory_space=pl.ANY)
    dma = pltpu.SemaphoreType.DMA
    return pl.pallas_call(
        partial(layer_kernel, late),
        out_shape=(
            jax.ShapeDtypeStruct((TOK, D), BF16),
            jax.ShapeDtypeStruct((HID, D), BF16),
        ),
        in_specs=[vmem] * 4 + [hbm] * 6,
        out_specs=(vmem, vmem),
        scratch_shapes=[
            pltpu.VMEM((4, 2, CAP, D), BF16),
            pltpu.VMEM((COLS, TOK), BF16),
            pltpu.VMEM((2, 2, 4, CAP, D), BF16),
            pltpu.VMEM((2, 3 * HID, D), BF16),
            pltpu.VMEM((4, 2 * HID, COLS), F32),
            pltpu.VMEM((HID, COLS), F32),
            pltpu.VMEM((2 * HID, COLS), BF16),
            pltpu.VMEM((HID, COLS), BF16),
            pltpu.VMEM((COLS, D), F32),
            pltpu.VMEM((2, HID, D), F32),
            pltpu.VMEM((HID, D), BF16),
            pltpu.VMEM((HID, D), BF16),
            pltpu.VMEM((4, CAP, D), BF16),
            pltpu.VMEM((4, CAP, D), BF16),
            pltpu.VMEM((4, CAP, D), BF16),
            pltpu.VMEM((4, CAP, D), BF16),
            pltpu.VMEM((len(late), HID, D), BF16),
            pltpu.VMEM((len(late), HID, D), BF16),
            pltpu.VMEM((3, HID, D), BF16),
            dma((4,)),
            dma((4,)),
            dma((4,)),
            dma((4,)),
            dma((3,)),
            dma((3,)),
            dma((len(CHUNKS),)),
            dma((len(CHUNKS),)),
            dma((4,)),
            dma((4,)),
            dma((4,)),
            dma((4,)),
            dma((len(late), len(CHUNKS))),
            dma((len(late), len(CHUNKS))),
            dma((3,)),
            dma((3,)),
        ],
        compiler_params=pltpu.CompilerParams(
            collective_id=number, has_side_effects=True, vmem_limit_bytes=56 * 2**20
        ),
        cost_estimate=pl.CostEstimate(
            flops=7 * 10**9, bytes_accessed=6 * 10**6, transcendentals=10**6
        ),
    )(*arrays)


def from_peer(state, bit):
    count = lax.axis_size("rep")
    pairs = [(source, source ^ (1 << bit)) for source in range(count)]
    return lax.ppermute(state, "rep", pairs)


def shards(
    tokens,
    cotangent,
    route_ids,
    route_weights,
    gate_weight,
    up_weight,
    down_weight,
    tracker,
    grad_prev,
    gossip_step,
):
    steps = jnp.clip(gossip_step, 0, 2)[None, :]
    code = jnp.sum(steps * jnp.array([[9, 3, 1]], jnp.int32), axis=1, keepdims=True)
    found = code == jnp.arange(27, dtype=jnp.int32)[None, :]
    choice = jnp.sum(jnp.where(found, jnp.array(CHOICES, jnp.int32), 0), axis=1)
    choice = lax.optimization_barrier(choice)
    early, pick = choice[0], choice[1]
    maybe = [lambda state: state] + [partial(from_peer, bit=bit) for bit in range(3)]
    peer = lax.switch(early, maybe, tracker[0])
    out, new = lax.switch(
        pick,
        [partial(layer, late, number) for number, late in enumerate(LATE)],
        tokens[0],
        cotangent[0],
        route_ids[0].T,
        route_weights[0].T,
        gate_weight[0].T,
        up_weight[0].T,
        down_weight[0],
        tracker[0],
        peer,
        grad_prev[0],
    )
    return (out[None], new[None])


def solution(mesh):
    rows = P("rep", "exp", None)
    cols = P("rep", None, "exp")
    in_specs = (rows, rows, rows, rows, cols, cols, rows, rows, rows, P())
    return jax.shard_map(
        shards, mesh=mesh, in_specs=in_specs, out_specs=(rows, rows), check_vma=False
    )
```

profile of v0, /device:TPU:121, one launch (start us, length us, event | category | flops | bytes accessed | tf_op | source)
XLA Modules:
  0.0 225.9 jit_solution(15723584843351050802)
XLA Ops:
  0.6 0.0 copy-start.5
  0.6 0.6 copy-done.5
  1.3 1.3 multiply_reduce_fusion
  2.6 0.6 iota_compare_fusion
  3.2 0.0 copy-start
  3.3 0.7 copy-done
  3.9 0.1 select_reduce_fusion
  4.0 0.6 fusion
  5.9 0.0 copy-start.1
  5.9 0.0 copy-start.2
  6.0 4.9 %conditional.2 = (bf16[352,1024]{1,0:T(8,128)(2,1)}) conditional(s32[]{:T(128)} %bitcast.46, bf16[352,1024]{1,0:T(8,128)(2,1)} %bitcast.53, bf16[352,1024]{1,0:T(8,128)(2,1)} %bitcast.54, bf16[352,1024]{1,0:T(8,128)(2,1)} %bitcast.55, bf16[352,1024]{1,0:T(8,128)(2,1)} %bitcast.56), branch_computations={%region_2.3_spmd, %region_3.4_spmd, %region_4.5_spmd, %region_5.6_... | conditional | bytes 2883632 | solution.py:511
  6.0 2.7 %collective-permute-start = (bf16[352,1024]{1,0:T(8,128)(2,1)}, bf16[352,1024]{1,0:T(8,128)(2,1)}, u32[]{:S(2)}, u32[]{:S(2)}) collective-permute-start(bf16[352,1024]{1,0:T(8,128)(2,1)} %param.1), channel_id=1, source_target_pairs={{0,16},{16,0},{32,48},{48,32},{64,80},{80,64},{96,112},{112,96},{1... | collective-permute-start | bytes 2162696 | tf_op jit(solution)/shard_map/cond/branch_1_fun/ppermute | solution.py:489
  8.7 2.1 collective-permute-done
  10.8 0.0 copy-start.3
  10.8 0.0 copy-start.4
  10.8 0.0 copy-done.1
  10.8 0.0 copy-done.2
  10.9 0.7 copy-done.3
  11.5 0.0 copy-done.4
  11.5 212.8 %conditional.3 = ((bf16[128,1024]{1,0:T(8,128)(2,1)S(1)}, bf16[352,1024]{1,0:T(8,128)(2,1)S(1)})) conditional(s32[]{:T(128)} %bitcast.36, (bf16[1,128,1024]{2,1,0:T(8,128)(2,1)}, bf16[1,128,1024]{2,1,0:T(8,128)(2,1)}, bf16[1,352,1024]{2,1,0:T(8,128)(2,1)S(1)}, bf16[1,352,1024]{2,1,0:T(8,128)(2,1)S(1)}, ...), branch_computations={%region_6.7_spmd, %region_7.8_spmd, %region_8.9_spmd, %region_9.10... | conditional | flops 7000000000 | bytes 6000008 | solution.py:512
  17.2 206.9 %branch_6_fun.1 = (bf16[128,1024]{1,0:T(8,128)(2,1)S(1)}, bf16[352,1024]{1,0:T(8,128)(2,1)S(1)}) custom-call(bf16[128,1024]{1,0:T(8,128)(2,1)} %bitcast.110, bf16[128,1024]{1,0:T(8,128)(2,1)} %bitcast.119, s32[2,128]{1,0:T(2,128)S(1)} %get-tuple-element.319.ids_ref, bf16[2,128]{1,0:T(2,128)(2,1)S(1)} %get-tuple-element.320.wts_ref, ...), custom_call_target="tpu_custom_call" | custom-call | flops 7000000000 | bytes 6000000 | tf_op jit(solution)/shard_map/cond/branch_6_fun/pallas_call | solution.py:432
  224.3 0.7 copy.38
  225.0 0.9 copy.39
Async XLA Ops:
  0.6 0.7 copy-start.5
  3.2 0.7 copy-start
  5.9 4.9 %copy-start.1 = (bf16[1,352,1024]{2,1,0:T(8,128)(2,1)S(1)}, bf16[1,352,1024]{2,1,0:T(8,128)(2,1)}, u32[]{:S(2)}) copy-start(bf16[1,352,1024]{2,1,0:T(8,128)(2,1)} %param.31) | copy-start | bytes 2162692
  5.9 4.9 %copy-start.2 = (bf16[1,352,1024]{2,1,0:T(8,128)(2,1)S(1)}, bf16[1,352,1024]{2,1,0:T(8,128)(2,1)}, u32[]{:S(2)}) copy-start(bf16[1,352,1024]{2,1,0:T(8,128)(2,1)} %param.33) | copy-start | bytes 2162692
  6.0 4.9 %collective-permute-start = (bf16[352,1024]{1,0:T(8,128)(2,1)}, bf16[352,1024]{1,0:T(8,128)(2,1)}, u32[]{:S(2)}, u32[]{:S(2)}) collective-permute-start(bf16[352,1024]{1,0:T(8,128)(2,1)} %param.1), channel_id=1, source_target_pairs={{0,16},{16,0},{32,48},{48,32},{64,80},{80,64},{96,112},{112,96},{1... | collective-permute-start | bytes 2162696 | tf_op jit(solution)/shard_map/cond/branch_1_fun/ppermute | solution.py:489
  10.8 0.7 copy-start.3
  10.8 0.7 copy-start.4
where the time goes:
time: 226 us
  Pallas kernels  207 us (92%)
  loops' own time  5.94 us (3%)
  local copies, waits for them, and re-layouts  4.16 us (2%)
  starting transfers between devices  2.72 us (1%)
    pallas_call x1, Pallas kernels, layer(): pl.pallas_call(partial(layer_kernel, late), out_shape=(jax.ShapeDtypeStru...  207 us
    another operation x1, loops' own time, shards(): lax.switch(pick, [partial(layer, late, number) for number, late in enumer...  5.91 us
  transfers between devices with their start and end apart: 1, of which 1 were waited for; matrix products, arithmetic and copies ran while one was open for 0% of the time, Pallas kernels for 0%

commit v1 on v0

--- a/solution.py
+++ b/solution.py
@@ -16,13 +16,9 @@
 HID = 352
 COLS = 4 * CAP
 ORDER = (1, 3, 2)
-CHUNKS = ((0, 96), (96, 96), (192, 80), (272, 80))
+CHUNKS = ((0, 96), (96, 80), (176, 96), (272, 80))
+HALF = HID // 2
 LATE = ((0,), (1,), (2,), (0, 1), (0, 2), (1, 0), (1, 2), (2, 0), (2, 1))
-ALL = [(a, b, c) for a in range(3) for b in range(3) for c in range(3)]
-CHOICES = (
-    [0 if a in (b, c) else a + 1 for a, b, c in ALL],
-    [LATE.index((b,) if b == c else (b, c)) for a, b, c in ALL],
-)
 F32 = jnp.float32
 BF16 = jnp.bfloat16
 NT = (((1,), (1,)), ((), ()))
@@ -43,8 +39,7 @@
     gate_ref,
     up_ref,
     down_ref,
-    tracker_ref,
-    peer_ref,
+    start_ref,
     prev_ref,
     out_ref,
     new_ref,
@@ -95,9 +90,13 @@
     def at_z(d):
         return 4 * ((z + d) % 4) + x
 
-    def across(bit):
-        step = 2**bit
-        return rep + step * (1 - 2 * ((rep // step) % 2))
+    def across(*bits):
+        return rep + sum(2**bit * (1 - 2 * ((rep // 2**bit) % 2)) for bit in bits)
+
+    hops = [across(bit) for bit in late]
+    if late == (2, 1):
+        hops[0] = across(1, 2)
+    halves = len(late) == 2 and late[1] == 0
 
     def send(src, dst, ss, rs, to, replica=None):
         return pltpu.make_async_remote_copy(
@@ -115,11 +114,11 @@
     ]
     keep = [
         pltpu.make_async_copy(ref, kept.at[i], kept_sem.at[i])
-        for i, ref in enumerate((tracker_ref, peer_ref, prev_ref))
+        for i, ref in enumerate((start_ref, prev_ref))
     ]
     barrier = pltpu.get_barrier_semaphore()
     peers = [(rep, at_z(1)), (rep, at_z(2)), (rep, at_z(3)), (rep, pair), (rep, mate)]
-    peers += [(across(bit), e) for bit in late]
+    peers += [(hop, e) for hop in hops]
     for to in peers:
         pl.semaphore_signal(
             barrier, inc=1, device_id=to, device_id_type=pl.DeviceIdType.MESH
@@ -218,7 +217,20 @@
     def m_copy(i, c):
         at = chunk(c)
         return send(
-            msend.at[i, at], mrecv.at[i, at], m_ss.at[i, c], m_rs.at[i, c], e, across(late[i])
+            msend.at[i, at],
+            mrecv.at[i, at],
+            m_ss.at[i, c],
+            m_rs.at[i, c],
+            e,
+            hops[1] if halves else hops[i],
+        )
+
+    def half_copy(j, passed, core):
+        at = pl.ds(pl.multiple_of(core * HALF + CHUNKS[j][0], 16), CHUNKS[j][1])
+        k = 2 * passed + j
+        source = mrecv if passed else msend
+        return send(
+            source.at[2, at], mrecv.at[2, at], m_ss.at[2, k], m_rs.at[2, k], e, hops[passed]
         )
 
     def each_tile(start, count, step, body):
@@ -287,12 +299,13 @@
         copy.wait()
 
     def begin(at):
-        share = (grads[0, at] + grecv[at].astype(F32) - kept[2, at].astype(F32)) / ROUNDS
-        mixed = (kept[0, at].astype(F32) + kept[1, at].astype(F32)) * 0.5
-        mixed = mixed + (share if len(late) == 2 else 2.0 * share)
+        share = (grads[0, at] + grecv[at].astype(F32) - kept[1, at].astype(F32)) / ROUNDS
+        mixed = kept[0, at].astype(F32) + (share if len(late) == 2 else 2.0 * share)
         grads[0, at] = share
         grads[1, at] = mixed
         msend[0, at] = mixed.astype(BF16)
+        if halves:
+            msend[1, at] = share.astype(BF16)
 
     for c, (start, size) in enumerate(CHUNKS):
         if c + 2 < len(CHUNKS):
@@ -301,6 +314,8 @@
         g_copy(c).wait_recv()
         each_tile(start, size // 16, 16, begin)
         m_copy(0, c).start()
+        if halves:
+            m_copy(1, c).start()
 
     def mixed_by(i, at):
         return (grads[1, at] + mrecv[i, at].astype(F32)) * 0.5 + grads[0, at]
@@ -316,7 +331,22 @@
             each_tile(start, size // 16, 16, body)
             m_copy(1, c).start()
 
-    if len(late) == 2 and late[0] == 0:
+    core = rep % 2
+
+    def meet(at):
+        mixed = (grads[1, at] + mrecv[0, at].astype(F32)) * 0.5
+        grads[0, at] = 1.5 * grads[0, at] + 0.5 * mrecv[1, at].astype(F32)
+        grads[1, at] = mixed
+        msend[2, at] = mixed.astype(BF16)
+
+    if halves:
+        for c, (start, size) in enumerate(CHUNKS):
+            m_copy(0, c).wait_recv()
+            m_copy(1, c).wait_recv()
+            each_tile(start, size // 16, 16, meet)
+        for j in range(2):
+            half_copy(j, 0, core).start()
+    elif len(late) == 2 and late[0] == 0:
         pass_on()
 
     def p_copy(d):
@@ -389,7 +419,11 @@
         if d != 0:
             r_copy(d).start()
 
-    if len(late) == 2 and late[0] != 0:
+    if halves:
+        for j in range(2):
+            half_copy(j, 0, core).wait_recv()
+            half_copy(j, 1, core).start()
+    elif len(late) == 2 and late[0] != 0:
         pass_on()
     for d in (1, 3, 2):
         r_copy(d).wait_recv()
@@ -401,13 +435,17 @@
         return carry
 
     lax.fori_loop(0, D // WIDE, collect, 0)
-    last = len(late) - 1
+    last = 2 if halves else len(late) - 1
+    if halves:
+        for j in range(2):
+            half_copy(j, 1, 1 - core).wait_recv()
 
     def finish(at):
         new_ref[at] = mixed_by(last, at).astype(BF16)
 
     for c, (start, size) in enumerate(CHUNKS):
-        m_copy(last, c).wait_recv()
+        if not halves:
+            m_copy(last, c).wait_recv()
         each_tile(start, size // 16, 16, finish)
 
     z_copy(2).wait_send()
@@ -418,6 +456,10 @@
     for d in range(4):
         a_copy(d).wait_send()
     w_copy(2).wait_send()
+    if halves:
+        for j in range(2):
+            half_copy(j, 0, core).wait_send()
+            half_copy(j, 1, core).wait_send()
     for c in range(len(CHUNKS)):
         if c >= len(CHUNKS) - 2:
             g_copy(c).wait_send()
@@ -429,13 +471,14 @@
     vmem = pl.BlockSpec(memory_space=pltpu.VMEM)
     hbm = pl.BlockSpec(memory_space=pl.ANY)
     dma = pltpu.SemaphoreType.DMA
+    slots = 3 if len(late) == 2 and late[1] == 0 else len(late)
     return pl.pallas_call(
         partial(layer_kernel, late),
         out_shape=(
             jax.ShapeDtypeStruct((TOK, D), BF16),
             jax.ShapeDtypeStruct((HID, D), BF16),
         ),
-        in_specs=[vmem] * 4 + [hbm] * 6,
+        in_specs=[vmem] * 4 + [hbm] * 5,
         out_specs=(vmem, vmem),
         scratch_shapes=[
             pltpu.VMEM((4, 2, CAP, D), BF16),
@@ -454,9 +497,9 @@
             pltpu.VMEM((4, CAP, D), BF16),
             pltpu.VMEM((4, CAP, D), BF16),
             pltpu.VMEM((4, CAP, D), BF16),
-            pltpu.VMEM((len(late), HID, D), BF16),
-            pltpu.VMEM((len(late), HID, D), BF16),
-            pltpu.VMEM((3, HID, D), BF16),
+            pltpu.VMEM((slots, HID, D), BF16),
+            pltpu.VMEM((slots, HID, D), BF16),
+            pltpu.VMEM((2, HID, D), BF16),
             dma((4,)),
             dma((4,)),
             dma((4,)),
@@ -469,8 +512,8 @@
             dma((4,)),
             dma((4,)),
             dma((4,)),
-            dma((len(late), len(CHUNKS))),
-            dma((len(late), len(CHUNKS))),
+            dma((slots, len(CHUNKS))),
+            dma((slots, len(CHUNKS))),
             dma((3,)),
             dma((3,)),
         ],
@@ -487,6 +530,22 @@
     count = lax.axis_size("rep")
     pairs = [(source, source ^ (1 << bit)) for source in range(count)]
     return lax.ppermute(state, "rep", pairs)
+
+
+def average(state, bit):
+    peer = from_peer(state, bit)
+    return ((state.astype(F32) + peer.astype(F32)) * 0.5).astype(BF16)
+
+
+def average_with_core(state, bit):
+    state = average(state, 0)
+    first = lax.axis_index("rep") % 2 == 0
+    top, low = state[:HALF], state[HALF:]
+    mine = from_peer(jnp.where(first, top, low), bit)
+    other = from_peer(mine, 0)
+    peer = jnp.where(first, jnp.stack([mine, other]), jnp.stack([other, mine]))
+    peer = peer.reshape(state.shape)
+    return ((state.astype(F32) + peer.astype(F32)) * 0.5).astype(BF16)
 
 
 def shards(
@@ -501,14 +560,21 @@
     grad_prev,
     gossip_step,
 ):
-    steps = jnp.clip(gossip_step, 0, 2)[None, :]
-    code = jnp.sum(steps * jnp.array([[9, 3, 1]], jnp.int32), axis=1, keepdims=True)
-    found = code == jnp.arange(27, dtype=jnp.int32)[None, :]
-    choice = jnp.sum(jnp.where(found, jnp.array(CHOICES, jnp.int32), 0), axis=1)
+    steps = jnp.clip(gossip_step, 0, 2)
+    place = lax.broadcasted_iota(jnp.int32, (3,), 0)
+    code = jnp.sum(steps * jnp.where(place == 0, 9, jnp.where(place == 1, 3, 1)), keepdims=True)
+    number = lax.broadcasted_iota(jnp.int32, (2, 32), 1)
+    s1, s2, s3 = number // 9, number // 3 % 3, number % 3
+    early = jnp.where((s1 == s2) | (s1 == s3), 0, s1 + 1)
+    early = jnp.where((early > 1) & ((s2 == 0) | (s3 == 0)), early + 2, early)
+    pick = jnp.where(s2 == s3, s2, 3 + 2 * s2 + jnp.where(s3 > s2, s3 - 1, s3))
+    table = jnp.where(lax.broadcasted_iota(jnp.int32, (2, 32), 0) == 0, early, pick)
+    choice = jnp.sum(jnp.where(number == code, table, 0), axis=1)
     choice = lax.optimization_barrier(choice)
     early, pick = choice[0], choice[1]
-    maybe = [lambda state: state] + [partial(from_peer, bit=bit) for bit in range(3)]
-    peer = lax.switch(early, maybe, tracker[0])
+    maybe = [lambda state: state] + [partial(average, bit=bit) for bit in range(3)]
+    maybe += [partial(average_with_core, bit=bit) for bit in (1, 2)]
+    start = lax.switch(early, maybe, tracker[0])
     out, new = lax.switch(
         pick,
         [partial(layer, late, number) for number, late in enumerate(LATE)],
@@ -519,8 +585,7 @@
         gate_weight[0].T,
         up_weight[0].T,
         down_weight[0],
-        tracker[0],
-        peer,
+        start,
         grad_prev[0],
     )
     return (out[None], new[None])

time: 226 us -> 165 us (0.73)
  the two profiles are of different devices: /device:TPU:121 before, /device:TPU:14 now
where the time goes in v1:
time: 165 us
  Pallas kernels  120 us (73%)
  starting transfers between devices  19.7 us (12%)
  waiting for transfers between devices  17 us (10%)
  local copies, waits for them, and re-layouts  2.9 us (2%)
  other arithmetic  2.34 us (1%)
  between operations  2.08 us (1%)
    pallas_call x1, Pallas kernels, layer(): pl.pallas_call(partial(layer_kernel, late), out_shape=(jax.ShapeDtypeStru...  120 us
    ppermute x3, starting transfers between devices, from_peer(): return lax.ppermute(state, 'rep', pairs)  19.7 us
    ppermute x3, waiting for transfers between devices, from_peer(): return lax.ppermute(state, 'rep', pairs)  17 us
  transfers between devices with their start and end apart: 3, of which 3 were waited for; matrix products, arithmetic and copies ran while one was open for 0% of the time, Pallas kernels for 0%

profile of v1, /device:TPU:14, one launch (start us, length us, event | category | flops | bytes accessed | tf_op | source)
XLA Modules:
  0.0 165.1 jit_solution(14789224188632939259)
XLA Ops:
  0.6 0.0 copy-start
  0.6 0.0 copy-start.5
  0.6 0.7 copy-done.5
  1.4 0.6 fusion.12
  2.0 0.7 compare_and_fusion.2
  2.7 0.2 select_reduce_fusion
  2.9 0.6 fusion.13
  4.8 0.0 copy-done
  4.8 0.0 copy-start.1
  4.8 0.0 copy-start.2
  4.8 0.0 copy-start.3
  4.8 0.0 copy-start.4
  4.9 0.0 copy-start.6
  4.9 37.6 %conditional.2 = (bf16[352,1024]{1,0:T(8,128)(2,1)S(1)}) conditional(s32[]{:T(128)} %bitcast.53, bf16[352,1024]{1,0:T(8,128)(2,1)S(1)} %bitcast.63, bf16[352,1024]{1,0:T(8,128)(2,1)S(1)} %bitcast.64, bf16[352,1024]{1,0:T(8,128)(2,1)S(1)} %bitcast.65, bf16[352,1024]{1,0:T(8,128)(2,1)S(1)} %bitcast.66, ...), branch_computations={%region_2.3_spmd, %region_3.4_spmd, %region_4.5_spmd, %region_5.6_... | conditional | flops 4866063 | bytes 12615960 | solution.py:577
  4.9 2.1 %collective-permute-start.6 = (bf16[352,1024]{1,0:T(8,128)(2,1)S(1)}, bf16[352,1024]{1,0:T(8,128)(2,1)S(1)}, u32[]{:S(2)}, u32[]{:S(2)}) collective-permute-start(bf16[352,1024]{1,0:T(8,128)(2,1)S(1)} %param.5), channel_id=1, source_target_pairs={{0,16},{16,0},{32,48},{48,32},{64,80},{80,64},{96,112},{112,96},{1... | collective-permute-start | bytes 2162696 | tf_op jit(solution)/shard_map/cond/branch_5_fun/ppermute | solution.py:532
  7.0 2.1 %collective-permute-done.6 = bf16[352,1024]{1,0:T(8,128)(2,1)S(1)} collective-permute-done((bf16[352,1024]{1,0:T(8,128)(2,1)S(1)}, bf16[352,1024]{1,0:T(8,128)(2,1)S(1)}, u32[]{:S(2)}, u32[]{:S(2)}) %collective-permute-start.6) | collective-permute-done | bytes 720928 | tf_op jit(solution)/shard_map/cond/branch_5_fun/ppermute | solution.py:532
  9.1 0.4 multiply_convert_fusion.4
  9.5 15.7 %collective-permute-start.7 = (bf16[176,1024]{1,0:T(8,128)(2,1)S(1)}, bf16[176,1024]{1,0:T(8,128)(2,1)S(1)}, u32[]{:S(2)}, u32[]{:S(2)}) collective-permute-start(bf16[176,1024]{1,0:T(8,128)(2,1)S(1)} %slice_select_fusion.1), channel_id=1, source_target_pairs={{0,64},{16,80},{32,96},{48,112},{64,0},{80,16},{96,32},{112,48},{1... | collective-permute-start | bytes 1081352 | tf_op jit(solution)/shard_map/cond/branch_5_fun/ppermute | solution.py:532
  25.3 13.2 %collective-permute-done.7 = bf16[176,1024]{1,0:T(8,128)(2,1)S(1)} collective-permute-done((bf16[176,1024]{1,0:T(8,128)(2,1)S(1)}, bf16[176,1024]{1,0:T(8,128)(2,1)S(1)}, u32[]{:S(2)}, u32[]{:S(2)}) %collective-permute-start.7) | collective-permute-done | bytes 360480 | tf_op jit(solution)/shard_map/cond/branch_5_fun/ppermute | solution.py:532
  38.5 1.9 %collective-permute-start.8 = (bf16[176,1024]{1,0:T(8,128)(2,1)S(1)}, bf16[176,1024]{1,0:T(8,128)(2,1)S(1)}, u32[]{:S(2)}, u32[]{:S(2)}) collective-permute-start(bf16[176,1024]{1,0:T(8,128)(2,1)S(1)} %collective-permute-done.7), channel_id=1, source_target_pairs={{0,16},{16,0},{32,48},{48,32},{64,80},{80,64},{96,112},{112,96},{1... | collective-permute-start | bytes 1081352 | tf_op jit(solution)/shard_map/cond/branch_5_fun/ppermute | solution.py:532
  40.4 1.6 collective-permute-done.8
  42.1 0.1 maximum_select_fusion.1
  42.2 0.3 fusion.3
  42.5 0.0 copy-done.1
  42.5 0.0 copy-done.2
  42.5 0.0 copy-done.3
  42.5 0.0 copy-done.4
  42.6 0.0 copy-done.6
  42.6 121.0 %conditional.3 = ((bf16[128,1024]{1,0:T(8,128)(2,1)S(1)}, bf16[352,1024]{1,0:T(8,128)(2,1)S(1)})) conditional(s32[]{:T(128)} %bitcast.44, (bf16[1,128,1024]{2,1,0:T(8,128)(2,1)S(1)}, bf16[1,128,1024]{2,1,0:T(8,128)(2,1)}, bf16[1,352,1024]{2,1,0:T(8,128)(2,1)S(1)}, bf16[1,352,1024]{2,1,0:T(8,128)(2,1)S(1)}, ...), branch_computations={%region_8.9_spmd, %region_9.10_spmd, %region_10.11_spmd, %region_1... | conditional | flops 7000000000 | bytes 6000008 | solution.py:578
  42.6 120.4 %branch_0_fun.1 = (bf16[128,1024]{1,0:T(8,128)(2,1)S(1)}, bf16[352,1024]{1,0:T(8,128)(2,1)S(1)}) custom-call(bf16[128,1024]{1,0:T(8,128)(2,1)S(1)} %bitcast.111, bf16[128,1024]{1,0:T(8,128)(2,1)} %bitcast.120, s32[2,128]{1,0:T(2,128)S(1)} %get-tuple-element.233.ids_ref, bf16[2,128]{1,0:T(2,128)(2,1)S(1)} %get-tuple-element.234.wts_ref, ...), custom_call_target="tpu_custom_call" | custom-call | flops 7000000000 | bytes 6000000 | tf_op jit(solution)/shard_map/cond/branch_0_fun/pallas_call | solution.py:475
  163.6 0.7 copy.40
  164.3 0.9 copy.41
  (6 shorter events, 0.1 us)
Async XLA Ops:
  0.6 4.2 %copy-start = (bf16[1,352,1024]{2,1,0:T(8,128)(2,1)S(1)}, bf16[1,352,1024]{2,1,0:T(8,128)(2,1)}, u32[]{:S(2)}) copy-start(bf16[1,352,1024]{2,1,0:T(8,128)(2,1)} %param.32) | copy-start | bytes 2162692
  0.6 0.7 copy-start.5
  4.8 37.7 %copy-start.1 = (bf16[1,352,1024]{2,1,0:T(8,128)(2,1)S(1)}, bf16[1,352,1024]{2,1,0:T(8,128)(2,1)}, u32[]{:S(2)}) copy-start(bf16[1,352,1024]{2,1,0:T(8,128)(2,1)} %param.31) | copy-start | bytes 2162692
  4.8 37.7 %copy-start.2 = (bf16[1,352,1024]{2,1,0:T(8,128)(2,1)S(1)}, bf16[1,352,1024]{2,1,0:T(8,128)(2,1)}, u32[]{:S(2)}) copy-start(bf16[1,352,1024]{2,1,0:T(8,128)(2,1)} %param.33) | copy-start | bytes 2162692
  4.8 37.7 %copy-start.3 = (bf16[1,128,1024]{2,1,0:T(8,128)(2,1)S(1)}, bf16[1,128,1024]{2,1,0:T(8,128)(2,1)}, u32[]{:S(2)}) copy-start(bf16[1,128,1024]{2,1,0:T(8,128)(2,1)} %param.25) | copy-start | bytes 786436
  4.8 37.7 %copy-start.4 = (s32[1,128,2]{1,2,0:T(2,128)S(1)}, s32[1,128,2]{1,2,0:T(2,128)}, u32[]{:S(2)}) copy-start(s32[1,128,2]{1,2,0:T(2,128)} %param.27) | copy-start | bytes 3076
  4.9 37.7 %copy-start.6 = (bf16[1,128,2]{1,2,0:T(2,128)(2,1)S(1)}, bf16[1,128,2]{1,2,0:T(2,128)(2,1)}, u32[]{:S(2)}) copy-start(bf16[1,128,2]{1,2,0:T(2,128)(2,1)} %param.28) | copy-start | bytes 1540
  4.9 4.2 %collective-permute-start.6 = (bf16[352,1024]{1,0:T(8,128)(2,1)S(1)}, bf16[352,1024]{1,0:T(8,128)(2,1)S(1)}, u32[]{:S(2)}, u32[]{:S(2)}) collective-permute-start(bf16[352,1024]{1,0:T(8,128)(2,1)S(1)} %param.5), channel_id=1, source_target_pairs={{0,16},{16,0},{32,48},{48,32},{64,80},{80,64},{96,112},{112,96},{1... | collective-permute-start | bytes 2162696 | tf_op jit(solution)/shard_map/cond/branch_5_fun/ppermute | solution.py:532
  9.5 29.0 %collective-permute-start.7 = (bf16[176,1024]{1,0:T(8,128)(2,1)S(1)}, bf16[176,1024]{1,0:T(8,128)(2,1)S(1)}, u32[]{:S(2)}, u32[]{:S(2)}) collective-permute-start(bf16[176,1024]{1,0:T(8,128)(2,1)S(1)} %slice_select_fusion.1), channel_id=1, source_target_pairs={{0,64},{16,80},{32,96},{48,112},{64,0},{80,16},{96,32},{112,48},{1... | collective-permute-start | bytes 1081352 | tf_op jit(solution)/shard_map/cond/branch_5_fun/ppermute | solution.py:532
  38.5 3.6 %collective-permute-start.8 = (bf16[176,1024]{1,0:T(8,128)(2,1)S(1)}, bf16[176,1024]{1,0:T(8,128)(2,1)S(1)}, u32[]{:S(2)}, u32[]{:S(2)}) collective-permute-start(bf16[176,1024]{1,0:T(8,128)(2,1)S(1)} %collective-permute-done.7), channel_id=1, source_target_pairs={{0,16},{16,0},{32,48},{48,32},{64,80},{80,64},{96,112},{112,96},{1... | collective-permute-start | bytes 1081352 | tf_op jit(solution)/shard_map/cond/branch_5_fun/ppermute | solution.py:532

commit v2 on v1

--- a/solution.py
+++ b/solution.py
@@ -425,6 +425,22 @@
             half_copy(j, 1, core).start()
     elif len(late) == 2 and late[0] != 0:
         pass_on()
+    def conclude():
+        last = 2 if halves else len(late) - 1
+        if halves:
+            for j in range(2):
+                half_copy(j, 1, 1 - core).wait_recv()
+
+        def finish(at):
+            new_ref[at] = mixed_by(last, at).astype(BF16)
+
+        for c, (start, size) in enumerate(CHUNKS):
+            if not halves:
+                m_copy(last, c).wait_recv()
+            each_tile(start, size // 16, 16, finish)
+
+    if late == (0,):
+        conclude()
     for d in (1, 3, 2):
         r_copy(d).wait_recv()
 
@@ -435,18 +451,8 @@
         return carry
 
     lax.fori_loop(0, D // WIDE, collect, 0)
-    last = 2 if halves else len(late) - 1
-    if halves:
-        for j in range(2):
-            half_copy(j, 1, 1 - core).wait_recv()
-
-    def finish(at):
-        new_ref[at] = mixed_by(last, at).astype(BF16)
-
-    for c, (start, size) in enumerate(CHUNKS):
-        if not halves:
-            m_copy(last, c).wait_recv()
-        each_tile(start, size // 16, 16, finish)
+    if late != (0,):
+        conclude()
 
     z_copy(2).wait_send()
     p_copy(3).wait_send()

time: 165 us -> 184 us (1.12)
  the two profiles are of different devices: /device:TPU:14 before, /device:TPU:42 now
where the time goes in v2:
time: 184 us; the launch traced here: 185 us
  Pallas kernels  122 us (66%)
  waiting for transfers between devices  36.1 us (20%)
  starting transfers between devices  18.8 us (10%)
  local copies, waits for them, and re-layouts  2.9 us (2%)
  other arithmetic  2.34 us (1%)
  between operations  2.08 us (1%)
    pallas_call x1, Pallas kernels, layer(): pl.pallas_call(partial(layer_kernel, late), out_shape=(jax.ShapeDtypeStru...  122 us
    ppermute x3, waiting for transfers between devices, from_peer(): return lax.ppermute(state, 'rep', pairs)  36.1 us
    ppermute x3, starting transfers between devices, from_peer(): return lax.ppermute(state, 'rep', pairs)  18.8 us
  transfers between devices with their start and end apart: 3, of which 3 were waited for; matrix products, arithmetic and copies ran while one was open for 0% of the time, Pallas kernels for 0%

profile of v2, /device:TPU:42, one launch (start us, length us, event | category | flops | bytes accessed | tf_op | source)
XLA Modules:
  0.0 185.2 jit_solution(846229312875298844)
XLA Ops:
  0.6 0.0 copy-start
  0.6 0.0 copy-start.5
  0.6 0.7 copy-done.5
  1.4 0.6 fusion.12
  2.0 0.7 compare_and_fusion.2
  2.7 0.2 select_reduce_fusion
  2.9 0.6 fusion.13
  4.8 0.0 copy-done
  4.8 0.0 copy-start.1
  4.8 0.0 copy-start.2
  4.8 0.0 copy-start.3
  4.8 0.0 copy-start.4
  4.9 0.0 copy-start.6
  4.9 55.8 %conditional.2 = (bf16[352,1024]{1,0:T(8,128)(2,1)S(1)}) conditional(s32[]{:T(128)} %bitcast.53, bf16[352,1024]{1,0:T(8,128)(2,1)S(1)} %bitcast.63, bf16[352,1024]{1,0:T(8,128)(2,1)S(1)} %bitcast.64, bf16[352,1024]{1,0:T(8,128)(2,1)S(1)} %bitcast.65, bf16[352,1024]{1,0:T(8,128)(2,1)S(1)} %bitcast.66, ...), branch_computations={%region_2.3_spmd, %region_3.4_spmd, %region_4.5_spmd, %region_5.6_... | conditional | flops 4866063 | bytes 12615960 | solution.py:583
  4.9 2.1 %collective-permute-start.6 = (bf16[352,1024]{1,0:T(8,128)(2,1)S(1)}, bf16[352,1024]{1,0:T(8,128)(2,1)S(1)}, u32[]{:S(2)}, u32[]{:S(2)}) collective-permute-start(bf16[352,1024]{1,0:T(8,128)(2,1)S(1)} %param.5), channel_id=1, source_target_pairs={{0,16},{16,0},{32,48},{48,32},{64,80},{80,64},{96,112},{112,96},{1... | collective-permute-start | bytes 2162696 | tf_op jit(solution)/shard_map/cond/branch_5_fun/ppermute | solution.py:538
  7.0 2.1 %collective-permute-done.6 = bf16[352,1024]{1,0:T(8,128)(2,1)S(1)} collective-permute-done((bf16[352,1024]{1,0:T(8,128)(2,1)S(1)}, bf16[352,1024]{1,0:T(8,128)(2,1)S(1)}, u32[]{:S(2)}, u32[]{:S(2)}) %collective-permute-start.6) | collective-permute-done | bytes 720928 | tf_op jit(solution)/shard_map/cond/branch_5_fun/ppermute | solution.py:538
  9.1 0.4 multiply_convert_fusion.4
  9.5 14.8 %collective-permute-start.7 = (bf16[176,1024]{1,0:T(8,128)(2,1)S(1)}, bf16[176,1024]{1,0:T(8,128)(2,1)S(1)}, u32[]{:S(2)}, u32[]{:S(2)}) collective-permute-start(bf16[176,1024]{1,0:T(8,128)(2,1)S(1)} %slice_select_fusion.1), channel_id=1, source_target_pairs={{0,64},{16,80},{32,96},{48,112},{64,0},{80,16},{96,32},{112,48},{1... | collective-permute-start | bytes 1081352 | tf_op jit(solution)/shard_map/cond/branch_5_fun/ppermute | solution.py:538
  24.4 32.3 %collective-permute-done.7 = bf16[176,1024]{1,0:T(8,128)(2,1)S(1)} collective-permute-done((bf16[176,1024]{1,0:T(8,128)(2,1)S(1)}, bf16[176,1024]{1,0:T(8,128)(2,1)S(1)}, u32[]{:S(2)}, u32[]{:S(2)}) %collective-permute-start.7) | collective-permute-done | bytes 360480 | tf_op jit(solution)/shard_map/cond/branch_5_fun/ppermute | solution.py:538
  56.6 1.9 %collective-permute-start.8 = (bf16[176,1024]{1,0:T(8,128)(2,1)S(1)}, bf16[176,1024]{1,0:T(8,128)(2,1)S(1)}, u32[]{:S(2)}, u32[]{:S(2)}) collective-permute-start(bf16[176,1024]{1,0:T(8,128)(2,1)S(1)} %collective-permute-done.7), channel_id=1, source_target_pairs={{0,16},{16,0},{32,48},{48,32},{64,80},{80,64},{96,112},{112,96},{1... | collective-permute-start | bytes 1081352 | tf_op jit(solution)/shard_map/cond/branch_5_fun/ppermute | solution.py:538
  58.5 1.6 collective-permute-done.8
  60.2 0.1 maximum_select_fusion.1
  60.3 0.3 fusion.3
  60.6 0.0 copy-done.1
  60.6 0.0 copy-done.2
  60.7 0.0 copy-done.3
  60.7 0.0 copy-done.4
  60.7 0.0 copy-done.6
  60.7 122.9 %conditional.3 = ((bf16[128,1024]{1,0:T(8,128)(2,1)S(1)}, bf16[352,1024]{1,0:T(8,128)(2,1)S(1)})) conditional(s32[]{:T(128)} %bitcast.44, (bf16[1,128,1024]{2,1,0:T(8,128)(2,1)S(1)}, bf16[1,128,1024]{2,1,0:T(8,128)(2,1)}, bf16[1,352,1024]{2,1,0:T(8,128)(2,1)S(1)}, bf16[1,352,1024]{2,1,0:T(8,128)(2,1)S(1)}, ...), branch_computations={%region_8.9_spmd, %region_9.10_spmd, %region_10.11_spmd, %region_1... | conditional | flops 7000000000 | bytes 6000008 | solution.py:584
  60.9 122.3 %branch_5_fun.1 = (bf16[128,1024]{1,0:T(8,128)(2,1)S(1)}, bf16[352,1024]{1,0:T(8,128)(2,1)S(1)}) custom-call(bf16[128,1024]{1,0:T(8,128)(2,1)S(1)} %bitcast.116, bf16[128,1024]{1,0:T(8,128)(2,1)} %bitcast.125, s32[2,128]{1,0:T(2,128)S(1)} %get-tuple-element.288.ids_ref, bf16[2,128]{1,0:T(2,128)(2,1)S(1)} %get-tuple-element.289.wts_ref, ...), custom_call_target="tpu_custom_call" | custom-call | flops 7000000000 | bytes 6000000 | tf_op jit(solution)/shard_map/cond/branch_5_fun/pallas_call | solution.py:481
  183.6 0.7 copy.40
  184.3 0.9 copy.41
  (6 shorter events, 0.1 us)
Async XLA Ops:
  0.6 4.2 %copy-start = (bf16[1,352,1024]{2,1,0:T(8,128)(2,1)S(1)}, bf16[1,352,1024]{2,1,0:T(8,128)(2,1)}, u32[]{:S(2)}) copy-start(bf16[1,352,1024]{2,1,0:T(8,128)(2,1)} %param.32) | copy-start | bytes 2162692
  0.6 0.7 copy-start.5
  4.8 55.8 %copy-start.1 = (bf16[1,352,1024]{2,1,0:T(8,128)(2,1)S(1)}, bf16[1,352,1024]{2,1,0:T(8,128)(2,1)}, u32[]{:S(2)}) copy-start(bf16[1,352,1024]{2,1,0:T(8,128)(2,1)} %param.31) | copy-start | bytes 2162692
  4.8 55.8 %copy-start.2 = (bf16[1,352,1024]{2,1,0:T(8,128)(2,1)S(1)}, bf16[1,352,1024]{2,1,0:T(8,128)(2,1)}, u32[]{:S(2)}) copy-start(bf16[1,352,1024]{2,1,0:T(8,128)(2,1)} %param.33) | copy-start | bytes 2162692
  4.8 55.8 %copy-start.3 = (bf16[1,128,1024]{2,1,0:T(8,128)(2,1)S(1)}, bf16[1,128,1024]{2,1,0:T(8,128)(2,1)}, u32[]{:S(2)}) copy-start(bf16[1,128,1024]{2,1,0:T(8,128)(2,1)} %param.25) | copy-start | bytes 786436
  4.8 55.8 %copy-start.4 = (s32[1,128,2]{1,2,0:T(2,128)S(1)}, s32[1,128,2]{1,2,0:T(2,128)}, u32[]{:S(2)}) copy-start(s32[1,128,2]{1,2,0:T(2,128)} %param.27) | copy-start | bytes 3076
  4.9 55.8 %copy-start.6 = (bf16[1,128,2]{1,2,0:T(2,128)(2,1)S(1)}, bf16[1,128,2]{1,2,0:T(2,128)(2,1)}, u32[]{:S(2)}) copy-start(bf16[1,128,2]{1,2,0:T(2,128)(2,1)} %param.28) | copy-start | bytes 1540
  4.9 4.2 %collective-permute-start.6 = (bf16[352,1024]{1,0:T(8,128)(2,1)S(1)}, bf16[352,1024]{1,0:T(8,128)(2,1)S(1)}, u32[]{:S(2)}, u32[]{:S(2)}) collective-permute-start(bf16[352,1024]{1,0:T(8,128)(2,1)S(1)} %param.5), channel_id=1, source_target_pairs={{0,16},{16,0},{32,48},{48,32},{64,80},{80,64},{96,112},{112,96},{1... | collective-permute-start | bytes 2162696 | tf_op jit(solution)/shard_map/cond/branch_5_fun/ppermute | solution.py:538
  9.5 47.1 %collective-permute-start.7 = (bf16[176,1024]{1,0:T(8,128)(2,1)S(1)}, bf16[176,1024]{1,0:T(8,128)(2,1)S(1)}, u32[]{:S(2)}, u32[]{:S(2)}) collective-permute-start(bf16[176,1024]{1,0:T(8,128)(2,1)S(1)} %slice_select_fusion.1), channel_id=1, source_target_pairs={{0,64},{16,80},{32,96},{48,112},{64,0},{80,16},{96,32},{112,48},{1... | collective-permute-start | bytes 1081352 | tf_op jit(solution)/shard_map/cond/branch_5_fun/ppermute | solution.py:538
  56.6 3.6 %collective-permute-start.8 = (bf16[176,1024]{1,0:T(8,128)(2,1)S(1)}, bf16[176,1024]{1,0:T(8,128)(2,1)S(1)}, u32[]{:S(2)}, u32[]{:S(2)}) collective-permute-start(bf16[176,1024]{1,0:T(8,128)(2,1)S(1)} %collective-permute-done.7), channel_id=1, source_target_pairs={{0,16},{16,0},{32,48},{48,32},{64,80},{80,64},{96,112},{112,96},{1... | collective-permute-start | bytes 1081352 | tf_op jit(solution)/shard_map/cond/branch_5_fun/ppermute | solution.py:538
